TPU v7x, 32 devices: a whole 2x2x4 slice. The times are simulated.
32 devices in a mesh: dom: 8 (over z, x), rep: 4 (over y, core).
Axes of the slice: x: 2, y: 2, z: 4, core: 2. Of those that a mesh axis runs over, the one named last changes fastest.
Arguments:
- feats: bfloat16 [128, 32768], P('rep', 'dom'), may hold values from -6 to 6
- grad_out: bfloat16 [128, 32768], P('rep', 'dom'), may hold values from -6 to 6
- w_self: bfloat16 [128, 128], replicated, may hold values from -0.5 to 0.5
- w_neigh: bfloat16 [128, 128], replicated, may hold values from -0.5 to 0.5
- bias: float32 [128], replicated, may hold values from -3 to 3
- requests: int32 [8, 8], P('dom'), may hold values from -1 to 31, as said below
- cross_peer: int32 [768], P('dom'), may hold values from 0 to 7, as said below
- cross_block: int32 [768], P('dom'), may hold values from 0 to 31
- cross_count: int32 [8], P('dom'), may hold values from 1 to 96, as said below
- cross_w: bfloat16 [768, 128, 128], P('dom'), may hold values from -0.25 to 0.25
- inner_src: int32 [128], P('dom'), may hold values from 0 to 31
- inner_dst: int32 [128], P('dom'), may hold values from 0 to 31
- inner_w: bfloat16 [128, 128, 128], P('dom'), may hold values from -0.25 to 0.25
Outputs:
- activated: bfloat16 [128, 32768], P('rep', 'dom')
- d_feats: bfloat16 [128, 32768], P('rep', 'dom')
- grad_self: float32 [128, 128], P('rep')
- grad_neigh: float32 [128, 128], P('rep')
- grad_bias: float32 [128], P('rep')
Inputs may be any that keep to these rules, and one draw needn't show every extreme that they name: requests[p, q] >= 0 exactly when some cross tile of partition q names p as its peer; requests[p, p] = -1. `cross_peer`: every cross tile, live or not, names a peer p with requests[p, own partition] >= 0, never its own partition. `cross_count`: every peer that a partition's tiles name is named by one of its live tiles.
All inputs are finite; a program needn't handle non-finite values.
Results may differ from a plain program's by a relative error of at most 0.0058.
Values may be sent and summed in bfloat16 or wider, within the bound.
A program may use at most 64 MiB of HBM per device.

v0:
```python
import math

import jax
import jax.numpy as jnp
from jax import lax
from jax.sharding import PartitionSpec as P

HIGH = lax.Precision.HIGHEST


def block_onehot(ids, count):
    return (ids[:, None] == jnp.arange(count, dtype=jnp.int32)[None, :]).astype(jnp.float32)


def aggregate(
    blocks,
    requests,
    cross_peer,
    cross_block,
    living,
    cross_w,
    inner_src,
    inner_dst,
    inner_w,
    backward,
):
    columns, block_count, blk_width = blocks.shape
    dom_count = requests.shape[1]
    wanted = requests[0]
    outgoing = jnp.take(blocks, jnp.maximum(wanted, 0), axis=1)
    outgoing = jnp.where((wanted >= 0)[None, :, None], outgoing, jnp.zeros_like(outgoing))
    arrived = lax.all_to_all(outgoing, "dom", split_axis=1, concat_axis=1, tiled=True)
    incoming = jnp.take(arrived, cross_peer, axis=1)
    own_rows = jnp.take(blocks, cross_block, axis=1)
    toward_own = jnp.einsum("ckj,kij->cki", incoming, cross_w, preferred_element_type=jnp.float32)
    toward_peer = jnp.einsum("cki,kij->kcj", own_rows, cross_w, preferred_element_type=jnp.float32)
    placing = block_onehot(cross_block, block_count) * living[:, None]
    summed = jnp.einsum("ckj,kb->cbj", toward_own, placing, precision=HIGH)
    outbound = jax.ops.segment_sum(
        toward_peer * living[:, None, None], cross_peer, num_segments=dom_count
    )
    returned = lax.all_to_all(outbound, "dom", split_axis=0, concat_axis=0, tiled=True)
    homing = block_onehot(wanted, block_count)
    summed = summed + jnp.einsum("qcj,qb->cbj", returned, homing, precision=HIGH)
    if backward:
        source = jnp.take(blocks, inner_dst, axis=1)
        moved = jnp.einsum("cki,kij->ckj", source, inner_w, preferred_element_type=jnp.float32)
        landing = block_onehot(inner_src, block_count)
    else:
        source = jnp.take(blocks, inner_src, axis=1)
        moved = jnp.einsum("ckj,kij->cki", source, inner_w, preferred_element_type=jnp.float32)
        landing = block_onehot(inner_dst, block_count)
    return summed + jnp.einsum("ckj,kb->cbj", moved, landing, precision=HIGH)


def contract_nodes(left_m, right_m):
    return lax.dot_general(
        left_m, right_m, (((1,), (1,)), ((), ())), preferred_element_type=jnp.float32
    )


def contract_rows(left_m, right_m):
    return lax.dot_general(
        left_m, right_m, (((0,), (0,)), ((), ())), preferred_element_type=jnp.float32
    )


def local(
    feats,
    grad_out,
    w_self,
    w_neigh,
    bias,
    requests,
    cross_peer,
    cross_block,
    cross_count,
    cross_w,
    inner_src,
    inner_dst,
    inner_w,
):
    columns, node_count = feats.shape
    blk_width = cross_w.shape[1]
    block_count = node_count // blk_width
    member = lax.axis_index("rep")
    out_rows = w_self.shape[1] // lax.axis_size("rep")
    living = (jnp.arange(cross_w.shape[0], dtype=jnp.int32) < cross_count[0]).astype(jnp.float32)

    def apply_graph(field, backward):
        summed = aggregate(
            field.reshape(columns, block_count, blk_width),
            requests,
            cross_peer,
            cross_block,
            living,
            cross_w,
            inner_src,
            inner_dst,
            inner_w,
            backward,
        )
        return summed.reshape(columns, node_count)

    neighbor = apply_graph(feats, False).astype(jnp.bfloat16)
    in_self = lax.dynamic_slice_in_dim(w_self, member * columns, columns, 0)
    in_neigh = lax.dynamic_slice_in_dim(w_neigh, member * columns, columns, 0)
    preact = lax.psum_scatter(
        contract_rows(in_self, feats) + contract_rows(in_neigh, neighbor),
        "rep",
        scatter_dimension=0,
        tiled=True,
    )
    preact = preact + lax.dynamic_slice_in_dim(bias, member * out_rows, out_rows, 0)[:, None]
    sigmoid_z = jax.nn.sigmoid(preact)
    activated = (preact * sigmoid_z).astype(jnp.bfloat16)
    slope = (grad_out.astype(jnp.float32) * sigmoid_z * (1.0 + preact * (1.0 - sigmoid_z))).astype(
        jnp.bfloat16
    )
    full_slope = lax.all_gather(slope, "rep", axis=0, tiled=True)
    self_part = contract_nodes(feats, full_slope)
    neigh_part = contract_nodes(neighbor, full_slope)
    bias_part = jnp.sum(slope.astype(jnp.float32), axis=1)
    grad_self, grad_neigh, grad_bias = lax.psum((self_part, neigh_part, bias_part), "dom")
    norm_scale = 1.0 / math.sqrt(node_count * lax.axis_size("dom"))
    back_agg = jnp.dot(in_neigh, full_slope, preferred_element_type=jnp.float32).astype(
        jnp.bfloat16
    )
    d_feats = (
        jnp.dot(in_self, full_slope, preferred_element_type=jnp.float32)
        + apply_graph(back_agg, True)
    ).astype(jnp.bfloat16)
    return (
        activated,
        d_feats,
        grad_self * norm_scale,
        grad_neigh * norm_scale,
        grad_bias * norm_scale,
    )


def solution(mesh):
    placed = (
        P("rep", "dom"),
        P("rep", "dom"),
        P(),
        P(),
        P(),
        P("dom", None),
        P("dom"),
        P("dom"),
        P("dom"),
        P("dom", None, None),
        P("dom"),
        P("dom"),
        P("dom", None, None),
    )
    return jax.shard_map(
        local,
        mesh=mesh,
        in_specs=placed,
        out_specs=(P("rep", "dom"), P("rep", "dom"), P("rep", None), P("rep", None), P("rep")),
        check_vma=False,
    )
```

profile of v0, /device:TPU:0, one launch (start us, length us, event | category | flops | bytes accessed | tf_op | source)
XLA Modules:
  0.0 211.0 jit_solution(8293394911787758166)
XLA Ops:
  7.2 0.0 copy-start
  7.2 0.8 broadcast_maximum_fusion
  8.0 0.8 broadcast_compare_fusion.1
  8.8 1.0 copy_bitcast_fusion.1
  9.8 0.6 gather_fusion
  10.4 0.7 bitcast_select_fusion.1
  11.1 7.3 %all-to-all-start = ((bf16[32,8,128]{2,0,1:T(8,128)(2,1)}), bf16[32,8,128]{2,0,1:T(8,128)(2,1)S(1)}, u32[]{:S(2)}, u32[]{:S(2)}) async-start(bf16[32,8,128]{2,0,1:T(8,128)(2,1)} %bitcast_select_fusion.1), calls=%async_computation | async-start | bytes 131072 | tf_op jit(solution)/shard_map/all_to_all | solution.py:32
  18.4 0.7 compare_select_fusion.2
  19.0 0.7 compare_and_fusion.2
  19.7 0.7 compare_select_fusion.1
  20.3 0.7 compare_and_fusion.1
  21.0 1.6 gather_fusion.2
  23.3 1.2 gather_fusion.3
  24.5 2.9 %fusion.65 = f32[128,4096]{1,0:T(8,128)} fusion(bf16[32,4096]{1,0:T(8,128)(2,1)} %param.21, bf16[128,128]{1,0:T(8,128)(2,1)} %param.23, s32[]{:T(128)S(6)} %select_n.39), kind=kOutput, calls=%fused_computation.94 | convolution fusion | flops 33554432 | bytes 2367492 | tf_op jit(solution)/shard_map/dot_general | solution.py:63
  27.4 0.4 convolution_bitcast_fusion.3
  27.8 0.0 copy-done.4
  27.8 2.1 %convolution_multiply_fusion.1 = f32[96,32,128]{2,1,0:T(8,128)} fusion(bf16[96,128,128]{2,1,0:T(8,128)(2,1)S(1)} %copy-done, bf16[96,32,128]{2,1,0:T(8,128)(2,1)S(1)} %copy-done.4, f32[96]{0:T(128)S(1)} %compare_convert_fusion, pred[96]{0:T(512)(128)(4,1)S(1)} %compare_and_fusion.2), kind=kOutput, calls=%fused_computation.19 | convolution fusion | flops 101449728 | bytes 5505504 | tf_op jit(solution)/shard_map/cki,kij->kcj/dot_general | solution.py:36
  30.0 0.7 broadcast.69.clone
  30.6 13.2 %scatter_fusion = f32[8,32,128]{2,1,0:T(8,128)} fusion(f32[8,32,128]{2,1,0:T(8,128)} %broadcast.69.clone, s32[96]{0:T(128)S(1)} %copy-done.13, f32[96,32,128]{2,1,0:T(8,128)} %convolution_multiply_fusion.1), kind=kCustom, calls=%fused_computation.8 | custom fusion | flops 393216 | bytes 4718976 | tf_op jit(solution)/shard_map/scatter-add | solution.py:39
  43.8 0.0 all-to-all-done
  43.8 6.0 %all-to-all-start.1 = ((f32[8,32,128]{2,1,0:T(8,128)}), f32[8,32,128]{2,1,0:T(8,128)}, u32[]{:S(2)}, u32[]{:S(2)}) async-start(f32[8,32,128]{2,1,0:T(8,128)} %scatter_fusion), calls=%async_computation.1 | async-start | bytes 262144 | tf_op jit(solution)/shard_map/all_to_all | solution.py:42
  49.8 0.0 reduce-scatter.2.cloned.1.call-start
  49.9 1.6 gather_fusion.1
  51.5 4.1 %convolution_bitcast_fusion.1 = f32[32,96,128]{2,0,1:T(8,128)} fusion(bf16[96,128,128]{2,1,0:T(8,128)(2,1)S(1)} %copy-done, bf16[96,32,128]{2,1,0:T(8,128)(2,1)} %gather_fusion.1, pred[96]{0:T(512)(128)(4,1)S(1)} %compare_and_fusion.3), kind=kOutput, calls=%fused_computation.21 | convolution fusion | flops 101056512 | bytes 5505120 | tf_op jit(solution)/shard_map/ckj,kij->cki/dot_general | solution.py:35
  55.6 1.7 all-to-all-done.1
  57.3 1.4 fusion.40
  58.7 0.0 copy-start.12
  58.7 3.3 %fusion.5 = f32[32,32,128]{2,0,1:T(8,128)S(1)} fusion(f32[32,32,128]{2,0,1:T(8,128)S(1)} %fusion.40, f32[32,96,128]{2,0,1:T(8,128)} %convolution_bitcast_fusion.1, f32[96]{0:T(128)S(1)} %compare_convert_fusion, s32[96]{0:T(128)S(1)} %copy-done.14), kind=kOutput, calls=%fused_computation.24 | convolution fusion | flops 151132160 | bytes 2622208 | tf_op jit(solution)/shard_map/ckj,kb->cbj/dot_general | solution.py:38
  62.0 0.5 fusion.11
  62.6 0.7 copy-done.5
  63.3 1.8 convolution_add_fusion
  65.1 0.0 reduce-scatter.2.cloned.1.call-update
  65.1 0.0 all-gather.2.cloned.1.call-start
  65.2 0.6 copy-done.21
  65.7 0.1 dynamic_slice.11
  65.8 30.5 %reduce-scatter.2.cloned.1.call-done = f32[32,4096]{1,0:T(8,128)} async-done(((f32[128,4096]{1,0:T(8,128)}), f32[32,4096]{1,0:T(8,128)}) %reduce-scatter.2.cloned.1.call-update) | async-done | bytes 524304 | tf_op jit(solution)/shard_map/reduce_scatter | solution.py:108
  96.3 2.3 %convert_reduce_fusion = (f32[32]{0:T(128)S(1)}, bf16[32,4096]{1,0:T(8,128)(2,1)}, bf16[32,4096]{1,0:T(8,128)(2,1)}) fusion(f32[32,4096]{1,0:T(8,128)} %reduce-scatter.2.cloned.1.call-done, f32[32]{0:T(128)S(1)} %dynamic_slice.11, bf16[32,4096]{1,0:T(8,128)(2,1)S(1)} %copy-done.11), kind=kLoop, calls=%fused_computation.43 | loop fusion | flops 1966048 | bytes 1310976 | tf_op jit(solution)/shard_map/reduce_sum | solution.py:123
  98.6 0.0 all-gather.2.cloned.1.call-update
  98.7 0.5 compare_and_fusion
  99.2 16.3 %all-gather.2.cloned.1.call-done = bf16[128,4096]{1,0:T(8,128)(2,1)} async-done(((bf16[32,4096]{1,0:T(8,128)(2,1)}), bf16[128,4096]{1,0:T(8,128)(2,1)}) %all-gather.2.cloned.1.call-update) | async-done | bytes 1048592 | tf_op jit(solution)/shard_map/all_gather | solution.py:120
  115.5 1.5 fusion.12
  117.1 1.6 gather_fusion.6
  118.7 0.6 gather_fusion.4
  119.2 3.3 %convolution_multiply_fusion = f32[96,32,128]{2,1,0:T(8,128)} fusion(bf16[96,128,128]{2,1,0:T(8,128)(2,1)S(1)} %copy-done, bf16[96,32,128]{2,1,0:T(8,128)(2,1)} %gather_fusion.6, f32[96]{0:T(128)S(1)} %compare_convert_fusion, pred[96]{0:T(512)(128)(4,1)S(1)} %compare_and_fusion.2), kind=kOutput, calls=%fused_computation.18 | convolution fusion | flops 101449728 | bytes 5505504 | tf_op jit(solution)/shard_map/cki,kij->kcj/dot_general | solution.py:36
  122.5 0.7 bitcast_select_fusion
  123.2 5.5 %all-to-all-start.2 = ((bf16[32,8,128]{2,0,1:T(8,128)(2,1)}), bf16[32,8,128]{2,0,1:T(8,128)(2,1)S(1)}, u32[]{:S(2)}, u32[]{:S(2)}) async-start(bf16[32,8,128]{2,0,1:T(8,128)(2,1)} %bitcast_select_fusion), calls=%async_computation.3 | async-start | bytes 131072 | tf_op jit(solution)/shard_map/all_to_all | solution.py:32
  128.7 1.2 gather_fusion.7
  130.0 0.7 broadcast.69
  130.6 13.2 %scatter_fusion.1 = f32[8,32,128]{2,1,0:T(8,128)} fusion(f32[8,32,128]{2,1,0:T(8,128)} %broadcast.69, s32[96]{0:T(128)S(1)} %copy-done.13, f32[96,32,128]{2,1,0:T(8,128)} %convolution_multiply_fusion), kind=kCustom, calls=%fused_computation.9 | custom fusion | flops 393216 | bytes 4718976 | tf_op jit(solution)/shard_map/scatter-add | solution.py:39
  143.8 2.2 %convolution_bitcast_fusion.2 = f32[32,16,128]{2,0,1:T(8,128)} fusion(bf16[16,128,128]{2,1,0:T(8,128)(2,1)} %param.33, bf16[16,32,128]{2,1,0:T(8,128)(2,1)} %gather_fusion.7, pred[16]{0:T(512)(128)(4,1)S(1)} %copy-done.20), kind=kOutput, calls=%fused_computation.28 | convolution fusion | flops 16842752 | bytes 917520 | tf_op jit(solution)/shard_map/cki,kij->ckj/dot_general | solution.py:47
  146.0 1.7 convolution_bitcast_fusion.4
  147.7 0.0 copy-done.1
  147.7 0.5 fusion.29
  148.2 38.0 %all-reduce = (f32[32,128]{1,0:T(8,128)S(1)}, f32[32,128]{1,0:T(8,128)S(1)}, f32[32]{0:T(128)S(1)}) all-reduce(f32[32,128]{1,0:T(8,128)S(1)} %convolution_bitcast_fusion.4, f32[32,128]{1,0:T(8,128)S(1)} %fusion.29, f32[32]{0:T(128)S(1)} %get-tuple-element.12), channel_id=1, replica_groups=mesh['dom'=8,'rep'=4] {'dom'}, use_global_device_ids=true, to_apply=%region_3.8 | all-reduce | flops 8224 | bytes 65792 | tf_op jit(solution)/shard_map/psum | solution.py:124
  186.2 0.6 broadcast_multiply_fusion
  186.8 0.5 broadcast_multiply_fusion.2
  187.3 3.6 %all-to-all-start.3 = ((f32[8,32,128]{2,1,0:T(8,128)}), f32[8,32,128]{2,1,0:T(8,128)S(1)}, u32[]{:S(2)}, u32[]{:S(2)}) async-start(f32[8,32,128]{2,1,0:T(8,128)} %scatter_fusion.1), calls=%async_computation.4 | async-start | bytes 262144 | tf_op jit(solution)/shard_map/all_to_all | solution.py:42
  190.9 1.6 gather_fusion.5
  192.4 4.1 %convolution_bitcast_fusion = f32[32,96,128]{2,0,1:T(8,128)} fusion(bf16[96,128,128]{2,1,0:T(8,128)(2,1)S(1)} %copy-done, bf16[96,32,128]{2,1,0:T(8,128)(2,1)} %gather_fusion.5, pred[96]{0:T(512)(128)(4,1)S(1)} %compare_and_fusion.3), kind=kOutput, calls=%fused_computation.20 | convolution fusion | flops 101056512 | bytes 5505120 | tf_op jit(solution)/shard_map/ckj,kij->cki/dot_general | solution.py:35
  196.6 1.4 all-to-all-done.3
  198.0 0.5 fusion.38
  198.5 3.2 %fusion.8 = f32[32,32,128]{2,0,1:T(8,128)S(1)} fusion(f32[32,32,128]{2,0,1:T(8,128)S(1)} %fusion.38, f32[32,96,128]{2,0,1:T(8,128)} %convolution_bitcast_fusion, f32[96]{0:T(128)S(1)} %compare_convert_fusion, s32[96]{0:T(128)S(1)} %copy-done.14), kind=kOutput, calls=%fused_computation.25 | convolution fusion | flops 151132160 | bytes 2622208 | tf_op jit(solution)/shard_map/ckj,kb->cbj/dot_general | solution.py:38
  201.7 0.6 convolution_add_fusion.2
  202.3 1.9 fusion
  (49 shorter events, 0.2 us)
Async XLA Ops:
  7.2 20.6 %copy-start = (bf16[96,128,128]{2,1,0:T(8,128)(2,1)S(1)}, bf16[96,128,128]{2,1,0:T(8,128)(2,1)}, u32[]{:S(2)}) copy-start(bf16[96,128,128]{2,1,0:T(8,128)(2,1)} %param.30) | copy-start | bytes 9437188
  7.2 16.1 %copy-start.13 = (s32[96]{0:T(128)S(1)}, s32[96]{0:T(128)}, u32[]{:S(2)}) copy-start(s32[96]{0:T(128)} %param.27) | copy-start | bytes 1156
  11.1 32.7 %all-to-all-start = ((bf16[32,8,128]{2,0,1:T(8,128)(2,1)}), bf16[32,8,128]{2,0,1:T(8,128)(2,1)S(1)}, u32[]{:S(2)}, u32[]{:S(2)}) async-start(bf16[32,8,128]{2,0,1:T(8,128)(2,1)} %bitcast_select_fusion.1), calls=%async_computation | async-start | bytes 131072 | tf_op jit(solution)/shard_map/all_to_all | solution.py:32
  24.5 2.9 %copy-start.8 = (bf16[16,128,128]{2,1,0:T(8,128)(2,1)S(1)}, bf16[16,128,128]{2,1,0:T(8,128)(2,1)}, u32[]{:S(2)}) copy-start(bf16[16,128,128]{2,1,0:T(8,128)(2,1)} %param.33) | copy-start | bytes 1572868
  24.5 2.9 %copy-start.10 = (bf16[16,32,128]{2,1,0:T(8,128)(2,1)S(1)}, bf16[16,32,128]{2,1,0:T(8,128)(2,1)}, u32[]{:S(2)}) copy-start(bf16[16,32,128]{2,1,0:T(8,128)(2,1)} %gather_fusion.3) | copy-start | bytes 393220
  24.5 3.3 %copy-start.4 = (bf16[96,32,128]{2,1,0:T(8,128)(2,1)S(1)}, bf16[96,32,128]{2,1,0:T(8,128)(2,1)}, u32[]{:S(2)}) copy-start(bf16[96,32,128]{2,1,0:T(8,128)(2,1)} %gather_fusion.2) | copy-start | bytes 2359300
  43.8 13.5 %all-to-all-start.1 = ((f32[8,32,128]{2,1,0:T(8,128)}), f32[8,32,128]{2,1,0:T(8,128)}, u32[]{:S(2)}, u32[]{:S(2)}) async-start(f32[8,32,128]{2,1,0:T(8,128)} %scatter_fusion), calls=%async_computation.1 | async-start | bytes 262144 | tf_op jit(solution)/shard_map/all_to_all | solution.py:42
  49.8 46.5 %reduce-scatter.2.cloned.1.call-start = ((), (), s32[]{:S(2)}) async-start(), calls=%async_computation.5 | async-start | bytes 2621440 | tf_op jit(solution)/shard_map/reduce_scatter | solution.py:108
  51.5 5.8 %copy-start.15 = (s32[1,8]{1,0:T(1,128)S(1)}, s32[1,8]{1,0:T(1,128)}, u32[]{:S(2)}) copy-start(s32[1,8]{1,0:T(1,128)} %param.26) | copy-start | bytes 100
  51.5 7.2 %copy-start.14 = (s32[96]{0:T(128)S(1)}, s32[96]{0:T(128)}, u32[]{:S(2)}) copy-start(s32[96]{0:T(128)} %param.28) | copy-start | bytes 1156
  57.3 4.7 %copy-start.17 = (s32[16]{0:T(128)S(1)}, s32[16]{0:T(128)}, u32[]{:S(2)}) copy-start(s32[16]{0:T(128)} %param.32) | copy-start | bytes 196
  58.7 4.6 %copy-start.3 = (f32[128,4096]{1,0:T(8,128)S(1)}, f32[128,4096]{1,0:T(8,128)}, u32[]{:S(2)}) copy-start(f32[128,4096]{1,0:T(8,128)} %fusion.65) | copy-start | bytes 6291460
  58.7 4.6 %copy-start.12 = (bf16[128,128]{1,0:T(8,128)(2,1)S(1)}, bf16[128,128]{1,0:T(8,128)(2,1)}, u32[]{:S(2)}) copy-start(bf16[128,128]{1,0:T(8,128)(2,1)} %param.24) | copy-start | bytes 98308
  62.6 0.7 copy-start.5
  65.1 0.7 copy-start.21
  65.1 31.3 %copy-start.11 = (bf16[32,4096]{1,0:T(8,128)(2,1)S(1)}, bf16[32,4096]{1,0:T(8,128)(2,1)}, u32[]{:S(2)}) copy-start(bf16[32,4096]{1,0:T(8,128)(2,1)} %param.22) | copy-start | bytes 786436
  65.1 33.6 %copy-start.18 = (s32[16]{0:T(128)S(1)}, s32[16]{0:T(128)}, u32[]{:S(2)}) copy-start(s32[16]{0:T(128)} %param.32) | copy-start | bytes 196
  65.1 50.4 %all-gather.2.cloned.1.call-start = ((), (), s32[]{:S(2)}) async-start(), calls=%async_computation.6 | async-start | bytes 1310720 | tf_op jit(solution)/shard_map/all_gather | solution.py:120
  123.2 64.1 %all-to-all-start.2 = ((bf16[32,8,128]{2,0,1:T(8,128)(2,1)}), bf16[32,8,128]{2,0,1:T(8,128)(2,1)S(1)}, u32[]{:S(2)}, u32[]{:S(2)}) async-start(bf16[32,8,128]{2,0,1:T(8,128)(2,1)} %bitcast_select_fusion), calls=%async_computation.3 | async-start | bytes 131072 | tf_op jit(solution)/shard_map/all_to_all | solution.py:32
  130.6 13.2 %copy-start.20 = (pred[16]{0:T(512)(128)(4,1)S(1)}, pred[16]{0:T(512)(128)(4,1)}, u32[]{:S(2)}) copy-start(pred[16]{0:T(512)(128)(4,1)} %compare_and_fusion) | copy-start | bytes 52
  130.6 15.4 %copy-start.7 = (bf16[32,4096]{1,0:T(8,128)(2,1)S(1)}, bf16[32,4096]{1,0:T(8,128)(2,1)}, u32[]{:S(2)}) copy-start(bf16[32,4096]{1,0:T(8,128)(2,1)} %param.21) | copy-start | bytes 786436
  143.8 3.9 %copy-start.1 = (bf16[128,4096]{1,0:T(8,128)(2,1)S(1)}, bf16[128,4096]{1,0:T(8,128)(2,1)}, u32[]{:S(2)}) copy-start(bf16[128,4096]{1,0:T(8,128)(2,1)} %all-gather.2.cloned.1.call-done) | copy-start | bytes 3145732
  143.8 3.9 %copy-start.6 = (bf16[32,32,128]{2,0,1:T(8,128)(2,1)S(1)}, bf16[32,32,128]{2,0,1:T(8,128)(2,1)}, u32[]{:S(2)}) copy-start(bf16[32,32,128]{2,0,1:T(8,128)(2,1)} %copy-done.5) | copy-start | bytes 786436
  187.3 10.7 %all-to-all-start.3 = ((f32[8,32,128]{2,1,0:T(8,128)}), f32[8,32,128]{2,1,0:T(8,128)S(1)}, u32[]{:S(2)}, u32[]{:S(2)}) async-start(f32[8,32,128]{2,1,0:T(8,128)} %scatter_fusion.1), calls=%async_computation.4 | async-start | bytes 262144 | tf_op jit(solution)/shard_map/all_to_all | solution.py:42
  192.4 5.5 %copy-start.16 = (s32[1,8]{1,0:T(1,128)S(1)}, s32[1,8]{1,0:T(1,128)}, u32[]{:S(2)}) copy-start(s32[1,8]{1,0:T(1,128)} %param.26) | copy-start | bytes 100
  196.6 5.1 %copy-start.9 = (f32[32,16,128]{2,0,1:T(8,128)S(1)}, f32[32,16,128]{2,0,1:T(8,128)}, u32[]{:S(2)}) copy-start(f32[32,16,128]{2,0,1:T(8,128)} %convolution_bitcast_fusion.2) | copy-start | bytes 786436
  196.6 5.1 %copy-start.19 = (s32[16]{0:T(128)S(1)}, s32[16]{0:T(128)}, u32[]{:S(2)}) copy-start(s32[16]{0:T(128)} %param.31) | copy-start | bytes 196
  198.5 3.8 %copy-start.2 = (bf16[128,4096]{1,0:T(8,128)(2,1)S(1)}, bf16[128,4096]{1,0:T(8,128)(2,1)}, u32[]{:S(2)}) copy-start(bf16[128,4096]{1,0:T(8,128)(2,1)} %all-gather.2.cloned.1.call-done) | copy-start | bytes 3145732
Sparse Core Ops, SparseCore 0:
  65.2 31.0 reduce-scatter.1
  98.8 16.7 all-gather.1
where the time goes:
time: 212 us; the launch traced here: 211 us
  waiting for transfers between devices  50.1 us (24%)
  blocking collectives  38 us (18%)
  other arithmetic  36 us (17%)
  matrix products  35.8 us (17%)
  starting transfers between devices  22.4 us (11%)
  between operations  15 us (7%)
  local copies, waits for them, and re-layouts  13.7 us (6%)
    psum x1, blocking collectives, local(): lax.psum((self_part, neigh_part, bias_part), 'dom')  38 us
    reduce_scatter x1, waiting for transfers between devices, local(): lax.psum_scatter(contract_rows(in_self, feats) + contract_rows(in_neigh,...  30.5 us
    scatter-add x2, other arithmetic, aggregate(): jax.ops.segment_sum(toward_peer * living[:, None, None], cross_peer, num_...  26.4 us
    all_gather x1, waiting for transfers between devices, local(): full_slope = lax.all_gather(slope, 'rep', axis=0, tiled=True)  16.3 us
    all_to_all x2, starting transfers between devices, aggregate(): lax.all_to_all(outgoing, 'dom', split_axis=1, concat_axis=1, tiled=True)  12.8 us
    all_to_all x2, starting transfers between devices, aggregate(): lax.all_to_all(outbound, 'dom', split_axis=0, concat_axis=0, tiled=True)  9.56 us
    dot_general x2, matrix products, aggregate(): jnp.einsum('ckj,kij->cki', incoming, cross_w, preferred_element_type=jnp....  8.2 us
    dot_general x2, matrix products, aggregate(): summed = jnp.einsum('ckj,kb->cbj', toward_own, placing, precision=HIGH)  6.47 us
  transfers between devices with their start and end apart: 6, of which 4 were waited for; matrix products, arithmetic and copies ran while one was open for 27% of the time, Pallas kernels for 0%

commit v1 on v0

v1 whole, which is shorter than its diff:
```python
import functools
import math

import jax
import jax.numpy as jnp
from jax import lax
from jax.experimental import pallas as pl
from jax.experimental.pallas import tpu as pltpu
from jax.sharding import PartitionSpec as P

MESH = pl.DeviceIdType.MESH
F32 = jnp.float32
BF16 = jnp.bfloat16


def each(first, count, step):
    if count <= 16:
        for i in range(first, count):
            step(i)
    else:

        def body(i, carry):
            step(i)
            return carry

        lax.fori_loop(first, count, body, 0)


def grouped(count, group, step):
    while count % group:
        group //= 2

    def body(i, carry):
        step([i * group + u for u in range(group)])
        return carry

    lax.fori_loop(0, count // group, body, 0)


def layer_kernel(
    sizes,
    links_ref,
    wanted_ref,
    peer_ref,
    block_ref,
    src_ref,
    dst_ref,
    feats_ref,
    gout_ref,
    wself_ref,
    wneigh_ref,
    bias_ref,
    cross_hbm,
    inner_hbm,
    act_ref,
    dfeats_ref,
    gself_ref,
    gneigh_ref,
    gbias_ref,
    cross_v,
    inner_v,
    far_send,
    far_recv_fwd,
    far_recv_bwd,
    out_send,
    ret_recv,
    chain,
    peer_chain,
    field,
    nbr,
    back,
    self_term,
    feats_n,
    gout_n,
    nbr_n,
    slope_n,
    act_n,
    back_n,
    self_n,
    grad_send,
    grad_recv,
    red_send,
    red_recv,
    red_all,
    load_sems,
    far_ss,
    far_rs,
    ret_ss,
    ret_rs,
    rep_ss,
    rep_rs,
    red_ss,
    red_rs,
    all_ss,
    all_rs,
):
    doms, reps, ct, it, nb, blk, cols, scale = sizes
    far_recv = (far_recv_fwd, far_recv_bwd)
    entries = it + ct + doms
    channels = cols * reps
    part = nb * blk // reps
    d = lax.axis_index("dom")
    r = lax.axis_index("rep")

    load_cross = pltpu.make_async_copy(cross_hbm, cross_v, load_sems.at[0])
    load_inner = pltpu.make_async_copy(inner_hbm, inner_v, load_sems.at[1])
    load_cross.start()
    load_inner.start()

    def dom_at(o):
        return lax.rem(d + o, doms)

    def rep_at(o):
        return lax.rem(r + o, reps)

    barrier = pltpu.get_barrier_semaphore()
    each(
        1,
        doms,
        lambda o: pl.semaphore_signal(
            barrier, inc=1, device_id={"dom": dom_at(o)}, device_id_type=MESH
        ),
    )
    each(
        1,
        reps,
        lambda o: pl.semaphore_signal(
            barrier, inc=1, device_id={"rep": rep_at(o)}, device_id_type=MESH
        ),
    )

    def lanes(i, width):
        return pl.ds(pl.multiple_of(i * width, width), width)

    def rows(i, height):
        return pl.ds(pl.multiple_of(i * height, height), height)

    def stage_far(turn, field):
        def stage(q):
            far_send[turn, q] = field[jnp.maximum(wanted_ref[0, q], 0)]

        each(0, doms, stage)
        far_recv[turn][d] = jnp.zeros((cols, blk), BF16)

    def far_copy(turn, o):
        q = dom_at(o)
        return pltpu.make_async_remote_copy(
            src_ref=far_send.at[turn, q],
            dst_ref=far_recv[turn].at[d],
            send_sem=far_ss.at[turn, o],
            recv_sem=far_rs.at[turn, o],
            device_id={"dom": q},
            device_id_type=MESH,
        )

    def ret_copy(turn, o):
        q = dom_at(o)
        return pltpu.make_async_remote_copy(
            src_ref=out_send.at[turn, q],
            dst_ref=ret_recv.at[turn, d],
            send_sem=ret_ss.at[turn, o],
            recv_sem=ret_rs.at[turn, o],
            device_id={"dom": q},
            device_id_type=MESH,
        )

    def to_nodes(slot, source, target, o):
        q = rep_at(o)
        return pltpu.make_async_remote_copy(
            src_ref=source.at[:, lanes(q, part)],
            dst_ref=target.at[rows(r, cols), :],
            send_sem=rep_ss.at[slot, o],
            recv_sem=rep_rs.at[slot, o],
            device_id={"rep": q},
            device_id_type=MESH,
        )

    def to_channels(slot, source, target, o):
        q = rep_at(o)
        return pltpu.make_async_remote_copy(
            src_ref=source.at[rows(q, cols), :],
            dst_ref=target.at[:, lanes(r, part)],
            send_sem=rep_ss.at[slot, o],
            recv_sem=rep_rs.at[slot, o],
            device_id={"rep": q},
            device_id_type=MESH,
        )

    def start_nodes(slot, source, target):
        each(1, reps, lambda o: to_nodes(slot, source, target, o).start())
        target[rows(r, cols), :] = source[:, lanes(r, part)]

    def wait_nodes(slot, source, target):
        each(1, reps, lambda o: to_nodes(slot, source, target, o).wait())

    def start_channels(slot, source, target):
        each(1, reps, lambda o: to_channels(slot, source, target, o).start())
        target[:, lanes(r, part)] = source[rows(r, cols), :]

    def wait_channels(slot, source, target):
        each(1, reps, lambda o: to_channels(slot, source, target, o).wait())

    def times(x, w):
        return jnp.dot(x, w, preferred_element_type=F32)

    def times_t(x, w):
        return lax.dot_general(x, w, (((1,), (1,)), ((), ())), preferred_element_type=F32)

    def add_peers(turn, field):
        def step(ks):
            moved = [times(field[block_ref[k]], cross_v[k]) for k in ks]
            for k, value in zip(ks, moved):
                peer_chain[k + 1] = peer_chain[links_ref[2, k]] + value

        grouped(ct, 8, step)

        def stage(q):
            out_send[turn, q] = peer_chain[links_ref[2, entries + q]]

        each(0, doms, stage)
        ret_recv[turn, d] = jnp.zeros((cols, blk), F32)
        each(1, doms, lambda o: ret_copy(turn, o).start())

    def add_inner(turn, field):
        def step(ks):
            if turn == 0:
                moved = [times_t(field[src_ref[k]], inner_v[k]) for k in ks]
            else:
                moved = [times(field[dst_ref[k]], inner_v[k]) for k in ks]
            for k, value in zip(ks, moved):
                chain[k + 1] = chain[links_ref[turn, k]] + value

        grouped(it, 8, step)

    def add_near(turn):
        def step(ks):
            moved = [times_t(far_recv[turn][peer_ref[k]], cross_v[k]) for k in ks]
            for k, value in zip(ks, moved):
                chain[it + k + 1] = chain[links_ref[turn, it + k]] + value

        grouped(ct, 8, step)

    def add_returned(turn):
        each(1, doms, lambda o: ret_copy(turn, o).wait())

        def step(q):
            e = it + ct + q
            chain[e + 1] = chain[links_ref[turn, e]] + ret_recv[turn, q]

        each(0, doms, step)

    chain[0] = jnp.zeros((cols, blk), F32)
    peer_chain[0] = jnp.zeros((cols, blk), F32)
    for b in range(nb):
        field[b] = feats_ref[:, b * blk : (b + 1) * blk]
    stage_far(0, field)
    pl.semaphore_wait(barrier, doms - 1 + reps - 1)
    each(1, doms, lambda o: far_copy(0, o).start())
    start_nodes(0, feats_ref, feats_n)
    start_nodes(1, gout_ref, gout_n)

    load_cross.wait()
    add_peers(0, field)
    load_inner.wait()
    add_inner(0, field)
    each(1, doms, lambda o: far_copy(0, o).wait())
    add_near(0)
    add_returned(0)
    for b in range(nb):
        nbr[:, b * blk : (b + 1) * blk] = chain[links_ref[0, entries + b]].astype(BF16)
    start_nodes(2, nbr, nbr_n)

    def back_copy(o):
        q = rep_at(o)
        return pltpu.make_async_remote_copy(
            src_ref=back_n.at[q],
            dst_ref=back.at[rows(r, nb // reps)],
            send_sem=rep_ss.at[3, o],
            recv_sem=rep_rs.at[3, o],
            device_id={"rep": q},
            device_id_type=MESH,
        )

    wide = min(256, part)
    bias_cols = jnp.transpose(jnp.broadcast_to(bias_ref[...], (blk, channels)))
    bias_cols = jnp.concatenate([bias_cols] * (wide // blk), axis=1)
    wself_t = jnp.transpose(wself_ref[...].astype(F32)).astype(BF16)
    wneigh_t = jnp.transpose(wneigh_ref[...].astype(F32)).astype(BF16)
    wait_nodes(0, feats_ref, feats_n)
    wait_nodes(1, gout_ref, gout_n)
    wait_nodes(2, nbr, nbr_n)
    for c in range(part // wide):
        at = slice(c * wide, (c + 1) * wide)
        preact = times(wself_t, feats_n[:, at]) + times(wneigh_t, nbr_n[:, at]) + bias_cols
        s = jax.nn.sigmoid(preact)
        act_n[:, at] = (preact * s).astype(BF16)
        slope = (gout_n[:, at].astype(F32) * s * (1.0 + preact * (1.0 - s))).astype(BF16)
        slope_n[:, at] = slope
        mixed = times(wneigh_ref[...], slope).astype(BF16)
        for q in range(reps):
            for u in range(wide // blk):
                back_n[q, c * (wide // blk) + u] = mixed[
                    q * cols : (q + 1) * cols, u * blk : (u + 1) * blk
                ]
    each(1, reps, lambda o: back_copy(o).start())
    back[rows(r, nb // reps)] = back_n[r]
    self_n[...] = times(wself_ref[...], slope_n[...]).astype(BF16)
    slope = slope_n[...]
    grads = (times_t(feats_n[...], slope), times_t(nbr_n[...], slope))
    ones = times_t(jnp.ones((16, part), BF16), slope)[:8]
    tall = 2 * cols + 8
    for q in range(reps):
        for i, grad in enumerate(grads):
            grad_send[q, i * cols : (i + 1) * cols] = grad[q * cols : (q + 1) * cols]
        grad_send[q, 2 * cols :] = ones

    def grad_copy(o):
        q = rep_at(o)
        return pltpu.make_async_remote_copy(
            src_ref=grad_send.at[q],
            dst_ref=grad_recv.at[r],
            send_sem=rep_ss.at[6, o],
            recv_sem=rep_rs.at[6, o],
            device_id={"rep": q},
            device_id_type=MESH,
        )

    each(1, reps, lambda o: back_copy(o).wait())
    stage_far(1, back)
    each(1, doms, lambda o: far_copy(1, o).start())
    each(1, reps, lambda o: grad_copy(o).start())
    grad_recv[r] = grad_send[r]
    add_peers(1, back)
    start_channels(4, self_n, self_term)
    start_channels(5, act_n, act_ref)

    add_inner(1, back)

    short = 2 * cols // doms
    split = short % 8 == 0 and short > 0
    each(1, reps, lambda o: grad_copy(o).wait())
    total = grad_recv[0]
    for q in range(1, reps):
        total = total + grad_recv[q]

    def red_copy(o):
        q = dom_at(o)
        return pltpu.make_async_remote_copy(
            src_ref=red_send.at[q] if split else red_send.at[0],
            dst_ref=red_recv.at[d],
            send_sem=red_ss.at[o],
            recv_sem=red_rs.at[o],
            device_id={"dom": q},
            device_id_type=MESH,
        )

    def all_copy(o):
        mine = red_all.at[rows(d, short), :]
        return pltpu.make_async_remote_copy(
            src_ref=mine,
            dst_ref=mine,
            send_sem=all_ss.at[o],
            recv_sem=all_rs.at[o],
            device_id={"dom": dom_at(o)},
            device_id_type=MESH,
        )

    if split:
        for q in range(doms):
            red_send[q, :short] = total[q * short : (q + 1) * short]
            red_send[q, short:] = total[2 * cols :]
        red_recv[d] = red_send[d]
    else:
        red_send[0] = total
        red_recv[d] = total
    each(1, doms, lambda o: red_copy(o).start())

    each(1, doms, lambda o: far_copy(1, o).wait())
    add_near(1)

    each(1, doms, lambda o: red_copy(o).wait())
    height = short + 8 if split else tall
    total = lax.fori_loop(
        0, doms, lambda q, acc: acc + red_recv[q], jnp.zeros((height, channels), F32)
    )
    gbias_ref[...] = total[height - 8 :] * scale
    if split:
        red_all[rows(d, short), :] = total[:short]
        each(1, doms, lambda o: all_copy(o).start())
    else:
        red_all[...] = total[: 2 * cols]

    add_returned(1)
    wait_channels(4, self_n, self_term)
    for b in range(nb):
        at = slice(b * blk, (b + 1) * blk)
        dfeats_ref[:, at] = (
            self_term[:, at].astype(F32) + chain[links_ref[1, entries + b]]
        ).astype(BF16)
    wait_channels(5, act_n, act_ref)
    if split:
        each(1, doms, lambda o: all_copy(o).wait())
    gself_ref[...] = red_all[:cols] * scale
    gneigh_ref[...] = red_all[cols:] * scale


def local(
    feats,
    grad_out,
    w_self,
    w_neigh,
    bias,
    requests,
    cross_peer,
    cross_block,
    cross_count,
    cross_w,
    inner_src,
    inner_dst,
    inner_w,
):
    cols, node_count = feats.shape
    ct, blk = cross_w.shape[:2]
    it = inner_w.shape[0]
    nb = node_count // blk
    doms = lax.axis_size("dom")
    reps = lax.axis_size("rep")
    channels = w_self.shape[1]
    part = node_count // reps
    scale = 1.0 / math.sqrt(node_count * doms)
    wanted = requests[0]

    entries = it + ct + doms
    live = jnp.arange(ct, dtype=jnp.int32) < cross_count[0]
    near = jnp.where(live, cross_block, -1)
    keys = jnp.stack(
        [
            jnp.concatenate([inner_dst, near, wanted]),
            jnp.concatenate([inner_src, near, wanted]),
            jnp.concatenate(
                [jnp.where(live, cross_peer, -1), jnp.full((it + doms,), -1, jnp.int32)]
            ),
        ]
    )
    ends = max(nb, doms)
    asked = jnp.concatenate(
        [keys, jnp.broadcast_to(jnp.arange(ends, dtype=jnp.int32), (3, ends))], axis=1
    )
    place = jnp.arange(entries, dtype=jnp.int32)
    limit = jnp.minimum(jnp.arange(entries + ends, dtype=jnp.int32), entries)
    same = (keys[:, None, :] == asked[:, :, None]) & (place[None, None, :] < limit[None, :, None])
    links = jnp.max(jnp.where(same, place[None, None, :] + 1, 0), axis=2)

    short = 2 * cols // doms
    split = short % 8 == 0 and short > 0
    red_rows = short + 8 if split else 2 * cols + 8
    smem = pl.BlockSpec(memory_space=pltpu.SMEM)
    vmem = pl.BlockSpec(memory_space=pltpu.VMEM)
    hbm = pl.BlockSpec(memory_space=pl.ANY)
    dma = pltpu.SemaphoreType.DMA
    act, dfeats, gself, gneigh, gbias = pl.pallas_call(
        functools.partial(layer_kernel, (doms, reps, ct, it, nb, blk, cols, scale)),
        out_shape=(
            jax.ShapeDtypeStruct((cols, node_count), BF16),
            jax.ShapeDtypeStruct((cols, node_count), BF16),
            jax.ShapeDtypeStruct((cols, channels), F32),
            jax.ShapeDtypeStruct((cols, channels), F32),
            jax.ShapeDtypeStruct((8, channels), F32),
        ),
        in_specs=[smem] * 6 + [vmem] * 5 + [hbm] * 2,
        out_specs=(vmem,) * 5,
        scratch_shapes=[
            pltpu.VMEM((ct, blk, blk), BF16),
            pltpu.VMEM((it, blk, blk), BF16),
            pltpu.VMEM((2, doms, cols, blk), BF16),
            pltpu.VMEM((doms, cols, blk), BF16),
            pltpu.VMEM((doms, cols, blk), BF16),
            pltpu.VMEM((2, doms, cols, blk), F32),
            pltpu.VMEM((2, doms, cols, blk), F32),
            pltpu.VMEM((entries + 1, cols, blk), F32),
            pltpu.VMEM((ct + 1, cols, blk), F32),
            pltpu.VMEM((nb, cols, blk), BF16),
            pltpu.VMEM((cols, node_count), BF16),
            pltpu.VMEM((nb, cols, blk), BF16),
            pltpu.VMEM((cols, node_count), BF16),
            pltpu.VMEM((channels, part), BF16),
            pltpu.VMEM((channels, part), BF16),
            pltpu.VMEM((channels, part), BF16),
            pltpu.VMEM((channels, part), BF16),
            pltpu.VMEM((channels, part), BF16),
            pltpu.VMEM((reps, nb // reps, cols, blk), BF16),
            pltpu.VMEM((channels, part), BF16),
            pltpu.VMEM((reps, 2 * cols + 8, channels), F32),
            pltpu.VMEM((reps, 2 * cols + 8, channels), F32),
            pltpu.VMEM((doms if split else 1, red_rows, channels), F32),
            pltpu.VMEM((doms, red_rows, channels), F32),
            pltpu.VMEM((2 * cols, channels), F32),
            dma((2,)),
            dma((2, doms)),
            dma((2, doms)),
            dma((2, doms)),
            dma((2, doms)),
            dma((7, reps)),
            dma((7, reps)),
            dma((doms,)),
            dma((doms,)),
            dma((doms,)),
            dma((doms,)),
        ],
        compiler_params=pltpu.CompilerParams(
            collective_id=0, has_side_effects=True, vmem_limit_bytes=40 * 1024 * 1024
        ),
    )(
        links,
        requests,
        cross_peer,
        cross_block,
        inner_src,
        inner_dst,
        feats,
        grad_out,
        w_self,
        w_neigh,
        bias.reshape(1, channels),
        cross_w,
        inner_w,
    )
    out_rows = channels // reps
    grad_bias = lax.dynamic_slice_in_dim(gbias[0], lax.axis_index("rep") * out_rows, out_rows, 0)
    return act, dfeats, gself, gneigh, grad_bias


def solution(mesh):
    placed = (
        P("rep", "dom"),
        P("rep", "dom"),
        P(),
        P(),
        P(),
        P("dom", None),
        P("dom"),
        P("dom"),
        P("dom"),
        P("dom", None, None),
        P("dom"),
        P("dom"),
        P("dom", None, None),
    )
    return jax.shard_map(
        local,
        mesh=mesh,
        in_specs=placed,
        out_specs=(P("rep", "dom"), P("rep", "dom"), P("rep", None), P("rep", None), P("rep")),
        check_vma=False,
    )
```

time: 212 us -> 54.1 us (0.26)
  waiting for transfers between devices: 50.1 us -> 0 us
  blocking collectives: 38 us -> 0 us
  Pallas kernels: 0 us -> 36.9 us
  matrix products: 35.8 us -> 0 us
  other arithmetic: 36 us -> 1.93 us
  starting transfers between devices: 22.4 us -> 0 us
  between operations: 15 us -> 1.35 us
    psum x1 -> x0, blocking collectives: 38 us -> none  [local(): lax.psum((self_part, neigh_part, bias_part), 'dom')]
    pallas_call x0 -> x1, Pallas kernels: none -> 36.9 us  [local(): pl.pallas_call(functools.partial(layer_kernel, (doms, reps, ct, it, nb, b...]
    dot_general x18 -> x0, matrix products: 35.8 us -> none  [the longest x2 8.2 us: aggregate(): jnp.einsum('ckj,kij->cki', incoming, cross_w, preferred_element_type=jnp....]
    reduce_scatter x1 -> x0, waiting for transfers between devices: 30.5 us -> none  [local(): lax.psum_scatter(contract_rows(in_self, feats) + contract_rows(in_neigh,...]
    scatter-add x2 -> x0, other arithmetic: 26.4 us -> none  [aggregate(): jax.ops.segment_sum(toward_peer * living[:, None, None], cross_peer, num_...]
    all_to_all x4 -> x0, starting transfers between devices: 22.3 us -> none  [the longest x2 12.8 us: aggregate(): lax.all_to_all(outgoing, 'dom', split_axis=1, concat_axis=1, tiled=True)]
    all_gather x1 -> x0, waiting for transfers between devices: 16.3 us -> none  [local(): full_slope = lax.all_gather(slope, 'rep', axis=0, tiled=True)]
    unnamed x44 -> x28, local copies, waits for them, and re-layouts: 1.38 us -> 12.9 us
  transfers between devices with their start and end apart: 6 -> 0, of which waited for: 4 -> 0; matrix products, arithmetic and copies ran while one was open for 27% -> 0% of each run, Pallas kernels for 0% -> 0%
where the time goes in v1:
time: 54.1 us; the launch traced here: 53.6 us
  Pallas kernels  36.9 us (68%)
  local copies, waits for them, and re-layouts  13.5 us (25%)
  other arithmetic  1.93 us (4%)
  between operations  1.35 us (2%)
    pallas_call x1, Pallas kernels, local(): pl.pallas_call(functools.partial(layer_kernel, (doms, reps, ct, it, nb, b...  36.9 us
    unnamed x28, local copies, waits for them, and re-layouts  12.9 us

profile of v1, /device:TPU:0, one launch (start us, length us, event | category | flops | bytes accessed | tf_op | source)
XLA Modules:
  0.0 53.6 jit_solution(8454381064943564244)
XLA Ops:
  1.3 0.7 %compare_select_fusion = (s32[96]{0:T(128)S(1)}, s32[96]{0:T(128)S(1)}) fusion(s32[96]{0:T(128)} %peer_ref.1, s32[]{:T(128)} %bitcast.11, s32[96]{0:T(128)} %block_ref.1), kind=kLoop, calls=%fused_computation.4 | loop fusion | flops 288 | bytes 1540 | tf_op jit(solution)/shard_map/jit(_where)/select_n | solution.py:441
  2.0 0.8 %add_bitcast_fusion = (s32[1,120]{1,0:T(1,128)S(1)}, s32[1,120]{1,0:T(1,128)S(1)}) fusion(s32[16]{0:T(128)} %dst_ref.1, s32[8]{0:T(128)} %bitcast.12, s32[96]{0:T(128)S(1)} %get-tuple-element.18, s32[16]{0:T(128)} %src_ref.1), kind=kLoop, calls=%fused_computation.7 | loop fusion | flops 480 | bytes 1504 | tf_op jit(solution)/shard_map/stack | solution.py:436
  2.7 0.1 pad_add_fusion
  2.8 0.1 iota_compare_fusion
  2.9 0.3 select_reduce_fusion.links_ref
  3.2 0.0 copy-start
  3.2 1.9 %copy-done = bf16[96,128,128]{2,1,0:T(8,128)(2,1)S(1)} copy-done((bf16[96,128,128]{2,1,0:T(8,128)(2,1)S(1)}, bf16[96,128,128]{2,1,0:T(8,128)(2,1)}, u32[]{:S(2)}) %copy-start) | copy-done | bytes 3145752
  5.1 0.0 copy-start.1
  5.1 1.0 %copy-done.1 = bf16[16,128,128]{2,1,0:T(8,128)(2,1)S(1)} copy-done((bf16[16,128,128]{2,1,0:T(8,128)(2,1)S(1)}, bf16[16,128,128]{2,1,0:T(8,128)(2,1)}, u32[]{:S(2)}) %copy-start.1) | copy-done | bytes 524312
  6.2 0.0 copy-start.2
  6.2 0.9 %copy-done.2 = bf16[32,4096]{1,0:T(8,128)(2,1)S(1)} copy-done((bf16[32,4096]{1,0:T(8,128)(2,1)S(1)}, bf16[32,4096]{1,0:T(8,128)(2,1)}, u32[]{:S(2)}) %copy-start.2) | copy-done | bytes 262168
  7.1 0.0 copy-start.3
  7.1 0.9 %copy-done.3 = bf16[32,4096]{1,0:T(8,128)(2,1)S(1)} copy-done((bf16[32,4096]{1,0:T(8,128)(2,1)S(1)}, bf16[32,4096]{1,0:T(8,128)(2,1)}, u32[]{:S(2)}) %copy-start.3) | copy-done | bytes 262168
  8.1 0.0 copy-start.4
  8.1 0.8 %copy-done.4 = bf16[128,128]{1,0:T(8,128)(2,1)S(1)} copy-done((bf16[128,128]{1,0:T(8,128)(2,1)S(1)}, bf16[128,128]{1,0:T(8,128)(2,1)}, u32[]{:S(2)}) %copy-start.4) | copy-done | bytes 32792
  8.8 0.0 copy-start.5
  8.8 0.8 %copy-done.5 = bf16[128,128]{1,0:T(8,128)(2,1)S(1)} copy-done((bf16[128,128]{1,0:T(8,128)(2,1)S(1)}, bf16[128,128]{1,0:T(8,128)(2,1)}, u32[]{:S(2)}) %copy-start.5) | copy-done | bytes 32792
  9.6 0.0 copy-start.6
  9.6 0.7 %copy-done.6 = s32[96]{0:T(128)S(1)} copy-done((s32[96]{0:T(128)S(1)}, s32[96]{0:T(128)}, u32[]{:S(2)}) %copy-start.6) | copy-done | bytes 408
  10.2 0.0 copy-start.7
  10.3 0.7 %copy-done.7 = s32[96]{0:T(128)S(1)} copy-done((s32[96]{0:T(128)S(1)}, s32[96]{0:T(128)}, u32[]{:S(2)}) %copy-start.7) | copy-done | bytes 408
  10.9 0.0 copy-start.8
  10.9 0.7 %copy-done.8 = s32[16]{0:T(128)S(1)} copy-done((s32[16]{0:T(128)S(1)}, s32[16]{0:T(128)}, u32[]{:S(2)}) %copy-start.8) | copy-done | bytes 88
  11.6 0.0 copy-start.9
  11.6 0.7 %copy-done.9 = s32[1,8]{1,0:T(1,128)S(1)} copy-done((s32[1,8]{1,0:T(1,128)S(1)}, s32[1,8]{1,0:T(1,128)}, u32[]{:S(2)}) %copy-start.9) | copy-done | bytes 56
  12.2 0.0 copy-start.10
  12.2 0.7 %copy-done.10 = s32[16]{0:T(128)S(1)} copy-done((s32[16]{0:T(128)S(1)}, s32[16]{0:T(128)}, u32[]{:S(2)}) %copy-start.10) | copy-done | bytes 88
  12.9 0.0 copy-start.11
  12.9 0.7 %copy-done.11 = f32[128]{0:T(128)S(1)} copy-done((f32[128]{0:T(128)S(1)}, f32[128]{0:T(128)}, u32[]{:S(2)}) %copy-start.11) | copy-done | bytes 536
  13.5 36.9 %shard_map.164 = (bf16[32,4096]{1,0:T(8,128)(2,1)S(1)}, bf16[32,4096]{1,0:T(8,128)(2,1)S(1)}, f32[32,128]{1,0:T(8,128)S(1)}, f32[32,128]{1,0:T(8,128)S(1)}, f32[8,128]{1,0:T(8,128)S(1)}) custom-call(s32[3,152]{1,0:T(4,128)S(1)} %select_reduce_fusion.links_ref, s32[1,8]{1,0:T(1,128)S(1)} %copy-done.9, s32[96]{0:T(128)S(1)} %copy-done.6, s32[96]{0:T(128)S(1)} %copy-done.7, ...), custom_call_target="tpu_custom_call" | custom-call | tf_op jit(solution)/shard_map/pallas_call | solution.py:461
  50.4 0.6 %dynamic-slice_bitcast_fusion = f32[32]{0:T(128)} fusion(f32[1,128]{1,0:T(1,128)S(1)} %slice.3, s32[]{:T(128)S(6)} %select_n.17), kind=kLoop, calls=%fused_computation.9 | loop fusion | bytes 260 | tf_op jit(solution)/shard_map/dynamic_slice | solution.py:529
  51.0 0.7 %copy.23 = bf16[32,4096]{1,0:T(8,128)(2,1)} copy(bf16[32,4096]{1,0:T(8,128)(2,1)S(1)} %get-tuple-element.24) | data formatting | bytes 524288
  51.7 0.7 %copy.24 = bf16[32,4096]{1,0:T(8,128)(2,1)} copy(bf16[32,4096]{1,0:T(8,128)(2,1)S(1)} %get-tuple-element.25) | data formatting | bytes 524288
  52.4 0.6 %copy.25 = f32[32,128]{1,0:T(8,128)} copy(f32[32,128]{1,0:T(8,128)S(1)} %get-tuple-element.26) | data formatting | bytes 32768
  53.0 0.6 %copy.26 = f32[32,128]{1,0:T(8,128)} copy(f32[32,128]{1,0:T(8,128)S(1)} %get-tuple-element.27) | data formatting | bytes 32768
  (6 shorter events, 0.0 us)
Async XLA Ops:
  3.2 1.9 %copy-start = (bf16[96,128,128]{2,1,0:T(8,128)(2,1)S(1)}, bf16[96,128,128]{2,1,0:T(8,128)(2,1)}, u32[]{:S(2)}) copy-start(bf16[96,128,128]{2,1,0:T(8,128)(2,1)} %cross_hbm.1) | copy-start | bytes 9437188
  5.1 1.0 %copy-start.1 = (bf16[16,128,128]{2,1,0:T(8,128)(2,1)S(1)}, bf16[16,128,128]{2,1,0:T(8,128)(2,1)}, u32[]{:S(2)}) copy-start(bf16[16,128,128]{2,1,0:T(8,128)(2,1)} %inner_hbm.1) | copy-start | bytes 1572868
  6.2 0.9 %copy-start.2 = (bf16[32,4096]{1,0:T(8,128)(2,1)S(1)}, bf16[32,4096]{1,0:T(8,128)(2,1)}, u32[]{:S(2)}) copy-start(bf16[32,4096]{1,0:T(8,128)(2,1)} %feats_ref.1) | copy-start | bytes 786436
  7.1 0.9 %copy-start.3 = (bf16[32,4096]{1,0:T(8,128)(2,1)S(1)}, bf16[32,4096]{1,0:T(8,128)(2,1)}, u32[]{:S(2)}) copy-start(bf16[32,4096]{1,0:T(8,128)(2,1)} %gout_ref.1) | copy-start | bytes 786436
  8.1 0.8 %copy-start.4 = (bf16[128,128]{1,0:T(8,128)(2,1)S(1)}, bf16[128,128]{1,0:T(8,128)(2,1)}, u32[]{:S(2)}) copy-start(bf16[128,128]{1,0:T(8,128)(2,1)} %wself_ref.1) | copy-start | bytes 98308
  8.8 0.8 %copy-start.5 = (bf16[128,128]{1,0:T(8,128)(2,1)S(1)}, bf16[128,128]{1,0:T(8,128)(2,1)}, u32[]{:S(2)}) copy-start(bf16[128,128]{1,0:T(8,128)(2,1)} %wneigh_ref.1) | copy-start | bytes 98308
  9.6 0.7 %copy-start.6 = (s32[96]{0:T(128)S(1)}, s32[96]{0:T(128)}, u32[]{:S(2)}) copy-start(s32[96]{0:T(128)} %peer_ref.1) | copy-start | bytes 1156
  10.2 0.7 %copy-start.7 = (s32[96]{0:T(128)S(1)}, s32[96]{0:T(128)}, u32[]{:S(2)}) copy-start(s32[96]{0:T(128)} %block_ref.1) | copy-start | bytes 1156
  10.9 0.7 %copy-start.8 = (s32[16]{0:T(128)S(1)}, s32[16]{0:T(128)}, u32[]{:S(2)}) copy-start(s32[16]{0:T(128)} %dst_ref.1) | copy-start | bytes 196
  11.6 0.7 %copy-start.9 = (s32[1,8]{1,0:T(1,128)S(1)}, s32[1,8]{1,0:T(1,128)}, u32[]{:S(2)}) copy-start(s32[1,8]{1,0:T(1,128)} %wanted_ref.1) | copy-start | bytes 100
  12.2 0.7 %copy-start.10 = (s32[16]{0:T(128)S(1)}, s32[16]{0:T(128)}, u32[]{:S(2)}) copy-start(s32[16]{0:T(128)} %src_ref.1) | copy-start | bytes 196
  12.9 0.7 %copy-start.11 = (f32[128]{0:T(128)S(1)}, f32[128]{0:T(128)}, u32[]{:S(2)}) copy-start(f32[128]{0:T(128)} %param.17) | copy-start | bytes 1540

commit v2 on v1

--- a/solution.py
+++ b/solution.py
@@ -11,6 +11,8 @@
 MESH = pl.DeviceIdType.MESH
 F32 = jnp.float32
 BF16 = jnp.bfloat16
+GROUP = 32
+LOADS = 12
 
 
 def each(first, count, step):
@@ -40,23 +42,19 @@
 def layer_kernel(
     sizes,
     links_ref,
-    wanted_ref,
-    peer_ref,
-    block_ref,
-    src_ref,
-    dst_ref,
+    feats_hbm,
+    gout_hbm,
+    wself_hbm,
+    wneigh_hbm,
+    bias_hbm,
+    cross_hbm,
+    inner_hbm,
+    field_out,
+    grad_out,
     feats_ref,
-    gout_ref,
     wself_ref,
     wneigh_ref,
     bias_ref,
-    cross_hbm,
-    inner_hbm,
-    act_ref,
-    dfeats_ref,
-    gself_ref,
-    gneigh_ref,
-    gbias_ref,
     cross_v,
     inner_v,
     far_send,
@@ -83,6 +81,7 @@
     red_recv,
     red_all,
     load_sems,
+    big_sems,
     far_ss,
     far_rs,
     ret_ss,
@@ -102,10 +101,6 @@
     d = lax.axis_index("dom")
     r = lax.axis_index("rep")
 
-    load_cross = pltpu.make_async_copy(cross_hbm, cross_v, load_sems.at[0])
-    load_inner = pltpu.make_async_copy(inner_hbm, inner_v, load_sems.at[1])
-    load_cross.start()
-    load_inner.start()
 
     def dom_at(o):
         return lax.rem(d + o, doms)
@@ -135,9 +130,37 @@
     def rows(i, height):
         return pl.ds(pl.multiple_of(i * height, height), height)
 
+    pairs = (
+        (feats_hbm, feats_ref),
+        (gout_hbm.at[:, lanes(r, part)], gout_n.at[rows(r, cols), :]),
+        (wself_hbm, wself_ref),
+        (wneigh_hbm, wneigh_ref),
+        (bias_hbm, bias_ref),
+    )
+    loads = [
+        pltpu.make_async_copy(source, target, load_sems.at[i])
+        for i, (source, target) in enumerate(pairs)
+    ]
+    loads[0].start()
+    bulk = ct // LOADS
+    big = [
+        pltpu.make_async_copy(
+            cross_hbm.at[pl.ds(i * bulk, bulk)],
+            cross_v.at[pl.ds(i * bulk, bulk)],
+            big_sems.at[i],
+        )
+        for i in range(LOADS)
+    ]
+    big.append(pltpu.make_async_copy(inner_hbm, inner_v, big_sems.at[LOADS]))
+    for load in big + loads[1:]:
+        load.start()
+    last = entries + max(nb, doms)
+    act_ref = field_out.at[0]
+    dfeats_ref = field_out.at[1]
+
     def stage_far(turn, field):
         def stage(q):
-            far_send[turn, q] = field[jnp.maximum(wanted_ref[0, q], 0)]
+            far_send[turn, q] = field[links_ref[0, last + it + ct + q]]
 
         each(0, doms, stage)
         far_recv[turn][d] = jnp.zeros((cols, blk), BF16)
@@ -208,11 +231,11 @@
 
     def add_peers(turn, field):
         def step(ks):
-            moved = [times(field[block_ref[k]], cross_v[k]) for k in ks]
+            moved = [times(field[links_ref[0, last + it + k]], cross_v[k]) for k in ks]
             for k, value in zip(ks, moved):
                 peer_chain[k + 1] = peer_chain[links_ref[2, k]] + value
 
-        grouped(ct, 8, step)
+        grouped(ct, GROUP, step)
 
         def stage(q):
             out_send[turn, q] = peer_chain[links_ref[2, entries + q]]
@@ -224,21 +247,21 @@
     def add_inner(turn, field):
         def step(ks):
             if turn == 0:
-                moved = [times_t(field[src_ref[k]], inner_v[k]) for k in ks]
+                moved = [times_t(field[links_ref[1, last + k]], inner_v[k]) for k in ks]
             else:
-                moved = [times(field[dst_ref[k]], inner_v[k]) for k in ks]
+                moved = [times(field[links_ref[0, last + k]], inner_v[k]) for k in ks]
             for k, value in zip(ks, moved):
                 chain[k + 1] = chain[links_ref[turn, k]] + value
 
-        grouped(it, 8, step)
+        grouped(it, 16, step)
 
     def add_near(turn):
         def step(ks):
-            moved = [times_t(far_recv[turn][peer_ref[k]], cross_v[k]) for k in ks]
+            moved = [times_t(far_recv[turn][links_ref[2, last + k]], cross_v[k]) for k in ks]
             for k, value in zip(ks, moved):
                 chain[it + k + 1] = chain[links_ref[turn, it + k]] + value
 
-        grouped(ct, 8, step)
+        grouped(ct, GROUP, step)
 
     def add_returned(turn):
         each(1, doms, lambda o: ret_copy(turn, o).wait())
@@ -251,17 +274,19 @@
 
     chain[0] = jnp.zeros((cols, blk), F32)
     peer_chain[0] = jnp.zeros((cols, blk), F32)
+    loads[0].wait()
     for b in range(nb):
         field[b] = feats_ref[:, b * blk : (b + 1) * blk]
     stage_far(0, field)
     pl.semaphore_wait(barrier, doms - 1 + reps - 1)
     each(1, doms, lambda o: far_copy(0, o).start())
     start_nodes(0, feats_ref, feats_n)
-    start_nodes(1, gout_ref, gout_n)
-
-    load_cross.wait()
+    each(1, reps, lambda o: to_nodes(1, gout_hbm, gout_n, o).start())
+
+    for load in big[:-1]:
+        load.wait()
     add_peers(0, field)
-    load_inner.wait()
+    big[-1].wait()
     add_inner(0, field)
     each(1, doms, lambda o: far_copy(0, o).wait())
     add_near(0)
@@ -270,24 +295,29 @@
         nbr[:, b * blk : (b + 1) * blk] = chain[links_ref[0, entries + b]].astype(BF16)
     start_nodes(2, nbr, nbr_n)
 
-    def back_copy(o):
+    wide = min(256, part)
+    step_blocks = wide // blk
+
+    def back_copy(c, o):
         q = rep_at(o)
-        return pltpu.make_async_remote_copy(
-            src_ref=back_n.at[q],
-            dst_ref=back.at[rows(r, nb // reps)],
-            send_sem=rep_ss.at[3, o],
-            recv_sem=rep_rs.at[3, o],
+        first = pl.multiple_of(r * (nb // reps) + c * step_blocks, step_blocks)
+        return pltpu.make_async_remote_copy(
+            src_ref=back_n.at[q, pl.ds(c * step_blocks, step_blocks)],
+            dst_ref=back.at[pl.ds(first, step_blocks)],
+            send_sem=rep_ss.at[7 + c, o],
+            recv_sem=rep_rs.at[7 + c, o],
             device_id={"rep": q},
             device_id_type=MESH,
         )
 
-    wide = min(256, part)
+    for load in loads[1:]:
+        load.wait()
     bias_cols = jnp.transpose(jnp.broadcast_to(bias_ref[...], (blk, channels)))
     bias_cols = jnp.concatenate([bias_cols] * (wide // blk), axis=1)
     wself_t = jnp.transpose(wself_ref[...].astype(F32)).astype(BF16)
     wneigh_t = jnp.transpose(wneigh_ref[...].astype(F32)).astype(BF16)
     wait_nodes(0, feats_ref, feats_n)
-    wait_nodes(1, gout_ref, gout_n)
+    wait_nodes(1, gout_hbm, gout_n)
     wait_nodes(2, nbr, nbr_n)
     for c in range(part // wide):
         at = slice(c * wide, (c + 1) * wide)
@@ -302,9 +332,8 @@
                 back_n[q, c * (wide // blk) + u] = mixed[
                     q * cols : (q + 1) * cols, u * blk : (u + 1) * blk
                 ]
-    each(1, reps, lambda o: back_copy(o).start())
+        each(1, reps, lambda o: back_copy(c, o).start())
     back[rows(r, nb // reps)] = back_n[r]
-    self_n[...] = times(wself_ref[...], slope_n[...]).astype(BF16)
     slope = slope_n[...]
     grads = (times_t(feats_n[...], slope), times_t(nbr_n[...], slope))
     ones = times_t(jnp.ones((16, part), BF16), slope)[:8]
@@ -325,17 +354,13 @@
             device_id_type=MESH,
         )
 
-    each(1, reps, lambda o: back_copy(o).wait())
+    each(1, reps, lambda o: grad_copy(o).start())
+    grad_recv[r] = grad_send[r]
+    self_n[...] = times(wself_ref[...], slope).astype(BF16)
+    for c in range(part // wide):
+        each(1, reps, lambda o: back_copy(c, o).wait())
     stage_far(1, back)
     each(1, doms, lambda o: far_copy(1, o).start())
-    each(1, reps, lambda o: grad_copy(o).start())
-    grad_recv[r] = grad_send[r]
-    add_peers(1, back)
-    start_channels(4, self_n, self_term)
-    start_channels(5, act_n, act_ref)
-
-    add_inner(1, back)
-
     short = 2 * cols // doms
     split = short % 8 == 0 and short > 0
     each(1, reps, lambda o: grad_copy(o).wait())
@@ -375,21 +400,26 @@
         red_recv[d] = total
     each(1, doms, lambda o: red_copy(o).start())
 
-    each(1, doms, lambda o: far_copy(1, o).wait())
-    add_near(1)
-
+    add_peers(1, back)
+    start_channels(4, self_n, self_term)
+    start_channels(5, act_n, act_ref)
+
+    add_inner(1, back)
     each(1, doms, lambda o: red_copy(o).wait())
     height = short + 8 if split else tall
     total = lax.fori_loop(
         0, doms, lambda q, acc: acc + red_recv[q], jnp.zeros((height, channels), F32)
     )
-    gbias_ref[...] = total[height - 8 :] * scale
+    mine = pltpu.roll(total[height - 8 :], lax.rem(channels - r * cols, channels), 1)
+    grad_out[2 * cols :] = mine * scale
     if split:
         red_all[rows(d, short), :] = total[:short]
         each(1, doms, lambda o: all_copy(o).start())
     else:
         red_all[...] = total[: 2 * cols]
 
+    each(1, doms, lambda o: far_copy(1, o).wait())
+    add_near(1)
     add_returned(1)
     wait_channels(4, self_n, self_term)
     for b in range(nb):
@@ -400,8 +430,7 @@
     wait_channels(5, act_n, act_ref)
     if split:
         each(1, doms, lambda o: all_copy(o).wait())
-    gself_ref[...] = red_all[:cols] * scale
-    gneigh_ref[...] = red_all[cols:] * scale
+    grad_out[: 2 * cols] = red_all[...] * scale
 
 
 def local(
@@ -450,6 +479,7 @@
     limit = jnp.minimum(jnp.arange(entries + ends, dtype=jnp.int32), entries)
     same = (keys[:, None, :] == asked[:, :, None]) & (place[None, None, :] < limit[None, :, None])
     links = jnp.max(jnp.where(same, place[None, None, :] + 1, 0), axis=2)
+    links = jnp.concatenate([links, jnp.maximum(keys, 0)], axis=1)
 
     short = 2 * cols // doms
     split = short % 8 == 0 and short > 0
@@ -458,18 +488,19 @@
     vmem = pl.BlockSpec(memory_space=pltpu.VMEM)
     hbm = pl.BlockSpec(memory_space=pl.ANY)
     dma = pltpu.SemaphoreType.DMA
-    act, dfeats, gself, gneigh, gbias = pl.pallas_call(
+    fields, grads = pl.pallas_call(
         functools.partial(layer_kernel, (doms, reps, ct, it, nb, blk, cols, scale)),
         out_shape=(
-            jax.ShapeDtypeStruct((cols, node_count), BF16),
-            jax.ShapeDtypeStruct((cols, node_count), BF16),
-            jax.ShapeDtypeStruct((cols, channels), F32),
-            jax.ShapeDtypeStruct((cols, channels), F32),
-            jax.ShapeDtypeStruct((8, channels), F32),
+            jax.ShapeDtypeStruct((2, cols, node_count), BF16),
+            jax.ShapeDtypeStruct((2 * cols + 8, channels), F32),
         ),
-        in_specs=[smem] * 6 + [vmem] * 5 + [hbm] * 2,
-        out_specs=(vmem,) * 5,
+        in_specs=[smem] + [hbm] * 7,
+        out_specs=(vmem,) * 2,
         scratch_shapes=[
+            pltpu.VMEM((cols, node_count), BF16),
+            pltpu.VMEM((channels, channels), BF16),
+            pltpu.VMEM((channels, channels), BF16),
+            pltpu.VMEM((1, channels), F32),
             pltpu.VMEM((ct, blk, blk), BF16),
             pltpu.VMEM((it, blk, blk), BF16),
             pltpu.VMEM((2, doms, cols, blk), BF16),
@@ -495,28 +526,24 @@
             pltpu.VMEM((doms if split else 1, red_rows, channels), F32),
             pltpu.VMEM((doms, red_rows, channels), F32),
             pltpu.VMEM((2 * cols, channels), F32),
-            dma((2,)),
+            dma((5,)),
+            dma((LOADS + 1,)),
             dma((2, doms)),
             dma((2, doms)),
             dma((2, doms)),
             dma((2, doms)),
-            dma((7, reps)),
-            dma((7, reps)),
+            dma((7 + part // min(256, part), reps)),
+            dma((7 + part // min(256, part), reps)),
             dma((doms,)),
             dma((doms,)),
             dma((doms,)),
             dma((doms,)),
         ],
         compiler_params=pltpu.CompilerParams(
-            collective_id=0, has_side_effects=True, vmem_limit_bytes=40 * 1024 * 1024
+            collective_id=0, has_side_effects=True, vmem_limit_bytes=58 * 1024 * 1024
         ),
     )(
         links,
-        requests,
-        cross_peer,
-        cross_block,
-        inner_src,
-        inner_dst,
         feats,
         grad_out,
         w_self,
@@ -525,9 +552,8 @@
         cross_w,
         inner_w,
     )
-    out_rows = channels // reps
-    grad_bias = lax.dynamic_slice_in_dim(gbias[0], lax.axis_index("rep") * out_rows, out_rows, 0)
-    return act, dfeats, gself, gneigh, grad_bias
+    gself, gneigh = grads[:cols], grads[cols : 2 * cols]
+    return fields[0], fields[1], gself, gneigh, grads[2 * cols, :cols]
 
 
 def solution(mesh):

time: 54.1 us -> 42.8 us (0.79)
  local copies, waits for them, and re-layouts: 13.5 us -> 4.39 us
  Pallas kernels: 36.9 us -> 34.1 us
  other arithmetic: 1.93 us -> 2.61 us
    unnamed x28 -> x0, local copies, waits for them, and re-layouts: 12.9 us -> none
    squeeze x0 -> x2, local copies, waits for them, and re-layouts: none -> 3.03 us  [local(): return (fields[0], fields[1], gself, gneigh, grads[2 * cols, :cols])]
    pallas_call x1, Pallas kernels: 36.9 us -> 34.1 us  [local(): pl.pallas_call(functools.partial(layer_kernel, (doms, reps, ct, it, nb, b...]
    slice x1, local copies, waits for them, and re-layouts: 0.01 us -> 1.35 us  [local(): gself, gneigh = (grads[:cols], grads[cols:2 * cols])]
    concatenate x0 -> x1, other arithmetic: none -> 0.67 us  [local(): links = jnp.concatenate([links, jnp.maximum(keys, 0)], axis=1)]
    dynamic_slice x1 -> x0, local copies, waits for them, and re-layouts: 0.59 us -> none  [local(): lax.dynamic_slice_in_dim(gbias[0], lax.axis_index('rep') * out_rows, out_...]
where the time goes in v2:
time: 42.8 us; the launch traced here: 42.4 us
  Pallas kernels  34.1 us (80%)
  local copies, waits for them, and re-layouts  4.39 us (10%)
  other arithmetic  2.61 us (6%)
  between operations  1.31 us (3%)
    pallas_call x1, Pallas kernels, local(): pl.pallas_call(functools.partial(layer_kernel, (doms, reps, ct, it, nb, b...  34.1 us
    squeeze x2, local copies, waits for them, and re-layouts, local(): return (fields[0], fields[1], gself, gneigh, grads[2 * cols, :cols])  3.03 us
    slice x1, local copies, waits for them, and re-layouts, local(): gself, gneigh = (grads[:cols], grads[cols:2 * cols])  1.35 us

profile of v2, /device:TPU:0, one launch (start us, length us, event | category | flops | bytes accessed | tf_op | source)
XLA Modules:
  0.0 42.4 jit_solution(70111527138837484)
XLA Ops:
  1.3 0.7 %compare_select_fusion = (s32[96]{0:T(128)S(1)}, s32[96]{0:T(128)S(1)}) fusion(s32[96]{0:T(128)} %param.19, s32[]{:T(128)} %bitcast.15, s32[96]{0:T(128)} %param.20), kind=kLoop, calls=%fused_computation.7 | loop fusion | flops 288 | bytes 1540 | tf_op jit(solution)/shard_map/jit(_where)/select_n | solution.py:470
  2.0 0.8 %add_bitcast_fusion = (s32[1,120]{1,0:T(1,128)S(1)}, s32[1,120]{1,0:T(1,128)S(1)}) fusion(s32[16]{0:T(128)} %param.24, s32[8]{0:T(128)} %bitcast.17, s32[96]{0:T(128)S(1)} %get-tuple-element.18, s32[16]{0:T(128)} %param.23), kind=kLoop, calls=%fused_computation.11 | loop fusion | flops 480 | bytes 1504 | tf_op jit(solution)/shard_map/stack | solution.py:465
  2.7 0.1 pad_add_fusion.1
  2.8 0.1 iota_compare_fusion
  2.9 0.3 select_reduce_fusion
  3.2 0.7 %pad_add_fusion.links_ref = s32[3,272]{1,0:T(4,128)} fusion(s32[3,120]{1,0:T(4,128)S(1)} %get-tuple-element.14, s32[3,152]{1,0:T(4,128)S(1)} %select_reduce_fusion), kind=kLoop, calls=%fused_computation.4 | loop fusion | flops 816 | bytes 6528 | tf_op jit(solution)/shard_map/concatenate | solution.py:482
  3.9 34.1 %shard_map.164 = (bf16[2,32,4096]{2,1,0:T(8,128)(2,1)}, f32[72,128]{1,0:T(8,128)}) custom-call(s32[3,272]{1,0:T(4,128)} %pad_add_fusion.links_ref, bf16[32,4096]{1,0:T(8,128)(2,1)} %feats_hbm.1, bf16[32,4096]{1,0:T(8,128)(2,1)} %gout_hbm.1, bf16[128,128]{1,0:T(8,128)(2,1)} %wself_hbm.1, bf16[128,128]{1,0:T(8,128)(2,1)} %wneigh_hbm.1, f32[1,128]{1,0:T(1,128)} %bitcast.16, ...), custom_call_target="tpu_custom_call" | custom-call | tf_op jit(solution)/shard_map/pallas_call | solution.py:491
  38.0 1.9 %slice_bitcast_fusion = (bf16[32,4096]{1,0:T(8,128)(2,1)}, bf16[32,4096]{1,0:T(8,128)(2,1)}) fusion(bf16[2,32,4096]{2,1,0:T(8,128)(2,1)} %get-tuple-element.7), kind=kLoop, calls=%fused_computation | loop fusion | bytes 1048576 | tf_op jit(solution)/shard_map/squeeze | solution.py:556
  39.9 1.2 %slice_bitcast_fusion.2 = f32[32]{0:T(128)} fusion(f32[72,128]{1,0:T(8,128)} %get-tuple-element.8), kind=kLoop, calls=%fused_computation.13 | loop fusion | bytes 256 | tf_op jit(solution)/shard_map/squeeze | solution.py:556
  41.1 1.3 %fusion = (f32[32,128]{1,0:T(8,128)}, f32[32,128]{1,0:T(8,128)}) fusion(f32[72,128]{1,0:T(8,128)} %get-tuple-element.8), kind=kLoop, calls=%fused_computation.16 | loop fusion | bytes 65536 | tf_op jit(solution)/shard_map/slice | solution.py:555
  (5 shorter events, 0.0 us)
